TPU v7x, 512 devices: a whole 4x4x16 slice. The times are simulated.
512 devices in a mesh: space: 32 (over x, z_hi, core), dp: 16 (over y, z_lo).
Axes of the slice: x: 4, y: 4, z: 16 (z_hi: 4, z_lo: 4; z = z_hi * 4 + z_lo), core: 2. Of those that a mesh axis runs over, the one named last changes fastest.
Arguments:
- tokens: bfloat16 [294912, 512], P(('space', 'dp')), may hold values from -6 to 6
- gain: float32 [512], replicated, may hold values from 0.25 to 1.75
- w_in: bfloat16 [32, 512, 1024], P('space'), may hold values from -0.25 to 0.25
- w_out: bfloat16 [32, 1024, 512], P('space'), may hold values from -0.1875 to 0.1875
- expert_ids: int32 [294912, 1], P(('space', 'dp')), may hold values from 0 to 31
- gate: bfloat16 [294912], P(('space', 'dp')), may hold values from 0.25 to 1
- grad_out: bfloat16 [294912, 512], P(('space', 'dp')), may hold values from -6 to 6
Outputs:
- grad_tokens: bfloat16 [294912, 512], P(('space', 'dp'))
- grad_gate: bfloat16 [294912], P(('space', 'dp'))
- grad_w_in: float32 [32, 512, 1024], P('space', 'dp')
- grad_w_out: float32 [32, 1024, 512], P('space', 'dp')
All inputs are finite; a program needn't handle non-finite values.
Results may differ from a plain program's by a relative error of at most 0.02.
Values may be sent and summed in bfloat16 or wider, within the bound.
A program may use at most 64 MiB of HBM per device.

v0:
```python
import jax
import jax.numpy as jnp
from jax import lax
from jax.sharding import PartitionSpec as P

epsilon = 1e-05


def normalize(tokens, gain):
    values = tokens.astype(jnp.float32)
    center = values - jnp.mean(values, axis=-1, keepdims=True)
    spread = lax.rsqrt(jnp.mean(center * center, axis=-1, keepdims=True) + epsilon)
    scaled = center * spread
    return (scaled, spread, (scaled * gain).astype(jnp.bfloat16))


def slot_ranks(routes, experts):
    onehot = (routes[:, None] == jnp.arange(experts, dtype=jnp.int32)[None, :]).astype(jnp.int32)
    before = jnp.cumsum(onehot, axis=0) - onehot
    return jnp.sum(before * onehot, axis=1)


def norm_backward(grad_norm, scaled, spread, gain):
    scaled_grad = grad_norm.astype(jnp.float32) * gain
    grad_mean = jnp.mean(scaled_grad, axis=-1, keepdims=True)
    grad_cross = jnp.mean(scaled_grad * scaled, axis=-1, keepdims=True)
    return spread * (scaled_grad - grad_mean - scaled * grad_cross)


def transpose_dot(left, right):
    return lax.dot_general(
        left, right, (((0,), (0,)), ((), ())), preferred_element_type=jnp.float32
    )


def right_dot(left, right):
    return lax.dot_general(
        left, right, (((1,), (1,)), ((), ())), preferred_element_type=jnp.float32
    )


def body(tokens, gain, w_in, w_out, expert_ids, gate, grad_out):
    sources = lax.axis_size("space")
    tok_rows = tokens.shape[0]
    model_width = tokens.shape[1]
    capacity = ((tok_rows * 5 // 4 + sources - 1) // sources + 7) // 8 * 8
    scaled, spread, normed = normalize(tokens, gain)
    routes = expert_ids[:, 0]
    slot_rank = slot_ranks(routes, sources)
    kept_mask = slot_rank < capacity
    target = jnp.where(kept_mask, routes * capacity + slot_rank, sources * capacity)
    row_index = jnp.minimum(target, sources * capacity - 1)
    grad_float = grad_out.astype(jnp.float32)
    weight_in = w_in[0]
    weight_out = w_out[0]

    def place_rows(rows):
        blank_rows = jnp.zeros((sources * capacity,) + rows.shape[1:], rows.dtype)
        placed = blank_rows.at[target].set(rows, mode="drop")
        return placed.reshape((sources, capacity) + rows.shape[1:])

    all_rows = sources * capacity
    delta = (gate[:, None].astype(jnp.float32) * grad_float).astype(jnp.bfloat16)
    normed_blocks, delta_blocks = (
        lax.all_to_all(place_rows(normed), "space", split_axis=0, concat_axis=0, tiled=True),
        lax.all_to_all(place_rows(delta), "space", split_axis=0, concat_axis=0, tiled=True),
    )
    normed_rows = normed_blocks.reshape(all_rows, model_width)
    delta_rows = delta_blocks.reshape(all_rows, model_width)
    preact = jnp.dot(normed_rows, weight_in, preferred_element_type=jnp.float32)
    act_float, gelu_back = jax.vjp(jax.nn.gelu, preact)
    activity = act_float.astype(jnp.bfloat16)
    token_out = jnp.dot(activity, weight_out, preferred_element_type=jnp.float32).astype(
        jnp.bfloat16
    )
    grad_activity = right_dot(delta_rows, weight_out)
    grad_preact = gelu_back(grad_activity)[0].astype(jnp.bfloat16)
    grad_normed = right_dot(grad_preact, weight_in).astype(jnp.bfloat16)
    activity, token_out, grad_preact, grad_normed = (activity, token_out, grad_preact, grad_normed)
    grad_back, out_back = (
        lax.all_to_all(
            grad_normed.reshape(sources, capacity, model_width),
            "space",
            split_axis=0,
            concat_axis=0,
            tiled=True,
        ),
        lax.all_to_all(
            token_out.reshape(sources, capacity, model_width),
            "space",
            split_axis=0,
            concat_axis=0,
            tiled=True,
        ),
    )
    token_grad = grad_back.reshape(sources * capacity, model_width)[row_index]
    token_result = out_back.reshape(sources * capacity, model_width)[row_index]
    product_sum = jnp.sum(grad_float * token_result.astype(jnp.float32), axis=1)
    grad_gate = jnp.where(kept_mask, product_sum, 0.0).astype(jnp.bfloat16)
    part_in = transpose_dot(normed_rows, grad_preact)
    part_out = transpose_dot(activity, delta_rows)
    grad_in, grad_out_weight = (
        lax.psum_scatter(
            part_in.astype(jnp.bfloat16), "dp", scatter_dimension=0, tiled=True
        ).astype(jnp.float32),
        lax.psum_scatter(
            part_out.astype(jnp.bfloat16), "dp", scatter_dimension=0, tiled=True
        ).astype(jnp.float32),
    )
    branch = jnp.where(kept_mask[:, None], norm_backward(token_grad, scaled, spread, gain), 0.0)
    grad_tokens = (grad_float + branch).astype(jnp.bfloat16)
    return (grad_tokens, grad_gate, grad_in[None], grad_out_weight[None])


def solution(mesh):
    placed = (
        P(("space", "dp"), None),
        P(),
        P("space", None, None),
        P("space", None, None),
        P(("space", "dp"), None),
        P(("space", "dp")),
        P(("space", "dp"), None),
    )
    return jax.shard_map(
        body,
        mesh=mesh,
        in_specs=placed,
        out_specs=(
            P(("space", "dp"), None),
            P(("space", "dp")),
            P("space", "dp", None),
            P("space", "dp", None),
        ),
        check_vma=False,
    )
```

profile of v0, /device:TPU:2, one launch (start us, length us, event | category | flops | bytes accessed | tf_op | source)
XLA Modules:
  0.0 369.9 jit_solution(5805009735525221346)
XLA Ops:
  13.4 7.5 %scatter_custom_fusion.1 = bf16[768,512]{1,0:T(8,128)(2,1)} fusion(s32[576]{0:T(1024)S(1)} %get-tuple-element.7, bf16[576,512]{1,0:T(8,128)(2,1)S(1)} %copy-done.1, f32[512]{0:T(512)} %param.8, f32[576]{0:T(1024)S(1)} %add_rsqrt_fusion, f32[576]{0:T(1024)S(1)} %broadcast_multiply_fusion.2, bf16[]{:T(256)} %constant.14.clone.1), kind=kCustom, calls=%fused_computation.46 | custom fusion | flops 1474560 | bytes 1386498 | tf_op jit(solution)/shard_map/scatter | solution.py:59
  20.9 18.2 %all-to-all-start.1 = ((bf16[32,24,512]{2,1,0:T(8,128)(2,1)}), bf16[32,24,512]{2,1,0:T(8,128)(2,1)S(1)}, u32[]{:S(2)}, u32[]{:S(2)}) async-start(bf16[32,24,512]{2,1,0:T(8,128)(2,1)} %bitcast.52), calls=%async_computation.1 | async-start | bytes 1572864 | tf_op jit(solution)/shard_map/all_to_all | solution.py:65
  39.2 9.1 %scatter_custom_fusion = bf16[768,512]{1,0:T(8,128)(2,1)} fusion(s32[576]{0:T(1024)S(1)} %get-tuple-element.7, bf16[576,512]{1,0:T(8,128)(2,1)S(1)} %copy-done.4, f32[576]{0:T(1024)S(1)} %convert_element_type.55, bf16[]{:T(256)} %constant.14.clone.1), kind=kCustom, calls=%fused_computation.45 | custom fusion | flops 884736 | bytes 1380354 | tf_op jit(solution)/shard_map/scatter | solution.py:59
  48.2 29.6 %all-to-all-done.1 = bf16[32,24,512]{2,1,0:T(8,128)(2,1)S(1)} async-done(((bf16[32,24,512]{2,1,0:T(8,128)(2,1)}), bf16[32,24,512]{2,1,0:T(8,128)(2,1)S(1)}, u32[]{:S(2)}, u32[]{:S(2)}) %all-to-all-start.1) | async-done | bytes 786464 | tf_op jit(solution)/shard_map/all_to_all | solution.py:65
  77.8 10.5 %all-to-all-start = ((bf16[32,24,512]{2,1,0:T(8,128)(2,1)}), bf16[32,24,512]{2,1,0:T(8,128)(2,1)}, u32[]{:S(2)}, u32[]{:S(2)}) async-start(bf16[32,24,512]{2,1,0:T(8,128)(2,1)} %bitcast.51), calls=%async_computation | async-start | bytes 1572864 | tf_op jit(solution)/shard_map/all_to_all | solution.py:66
  88.4 2.2 fusion.23
  90.6 1.7 copy-done.2
  92.2 2.0 convolution_convert_fusion.2
  94.3 22.5 %all-to-all-done = bf16[32,24,512]{2,1,0:T(8,128)(2,1)} async-done(((bf16[32,24,512]{2,1,0:T(8,128)(2,1)}), bf16[32,24,512]{2,1,0:T(8,128)(2,1)}, u32[]{:S(2)}, u32[]{:S(2)}) %all-to-all-start) | async-done | bytes 786464 | tf_op jit(solution)/shard_map/all_to_all | solution.py:66
  116.8 20.2 %all-to-all-start.3 = ((bf16[32,24,512]{2,1,0:T(8,128)(2,1)}), bf16[32,24,512]{2,1,0:T(8,128)(2,1)S(1)}, u32[]{:S(2)}, u32[]{:S(2)}) async-start(bf16[32,24,512]{2,1,0:T(8,128)(2,1)} %bitcast.54), calls=%async_computation.3 | async-start | bytes 1572864 | tf_op jit(solution)/shard_map/all_to_all | solution.py:88
  137.0 4.4 %convolution_convert_fusion = bf16[1024,512]{1,0:T(8,128)(2,1)} fusion(bf16[768,512]{1,0:T(8,128)(2,1)} %bitcast.2, f32[768,1024]{1,0:T(8,128)} %copy-done.2), kind=kOutput, calls=%fused_computation.17 | convolution fusion | flops 812908544 | bytes 4980736 | tf_op jit(solution)/shard_map/dot_general | solution.py:31
  141.5 4.5 %fusion.6 = bf16[768,1024]{1,0:T(8,128)(2,1)S(1)} fusion(f32[768,1024]{1,0:T(8,128)} %copy-done.2, bf16[768,512]{1,0:T(8,128)(2,1)} %bitcast.2, bf16[1,1024,512]{2,1,0:T(8,128)(2,1)S(1)} %copy-done), kind=kOutput, calls=%fused_computation.12 | convolution fusion | flops 821035008 | bytes 6553600 | tf_op jit(solution)/shard_map/dot_general | solution.py:37
  147.2 1.9 convolution_convert_fusion.3
  149.1 13.4 %all-to-all-done.3 = bf16[32,24,512]{2,1,0:T(8,128)(2,1)S(1)} async-done(((bf16[32,24,512]{2,1,0:T(8,128)(2,1)}), bf16[32,24,512]{2,1,0:T(8,128)(2,1)S(1)}, u32[]{:S(2)}, u32[]{:S(2)}) %all-to-all-start.3) | async-done | bytes 786464 | tf_op jit(solution)/shard_map/all_to_all | solution.py:88
  162.4 20.0 %all-to-all-start.2 = ((bf16[32,24,512]{2,1,0:T(8,128)(2,1)}), bf16[32,24,512]{2,1,0:T(8,128)(2,1)S(1)}, u32[]{:S(2)}, u32[]{:S(2)}) async-start(bf16[32,24,512]{2,1,0:T(8,128)(2,1)} %bitcast.53), calls=%async_computation.2 | async-start | bytes 1572864 | tf_op jit(solution)/shard_map/all_to_all | solution.py:81
  182.5 3.6 convolution_convert_fusion.1
  186.2 75.6 %reduce-scatter.5.cloned.1.call-done = bf16[64,512]{1,0:T(8,128)(2,1)} async-done(((bf16[1024,512]{1,0:T(8,128)(2,1)}), bf16[64,512]{1,0:T(8,128)(2,1)}) %reduce-scatter.5.cloned.1.call-update) | async-done | bytes 65552 | tf_op jit(solution)/shard_map/reduce_scatter | solution.py:106
  261.8 1.5 bitcast_convert_fusion
  263.3 87.1 %reduce-scatter.3.cloned.1.call-done = bf16[32,1024]{1,0:T(8,128)(2,1)} async-done(((bf16[512,1024]{1,0:T(8,128)(2,1)}), bf16[32,1024]{1,0:T(8,128)(2,1)}) %reduce-scatter.3.cloned.1.call-update) | async-done | bytes 65552 | tf_op jit(solution)/shard_map/reduce_scatter | solution.py:103
  350.4 1.5 bitcast_convert_fusion.1
  351.9 3.2 gather_fusion.1
  355.2 1.5 fusion.20
  357.3 2.7 gather_fusion
  360.6 2.4 fusion.19
  (40 shorter events, 8.6 us)
Async XLA Ops:
  7.2 85.1 %copy-start = (bf16[1,1024,512]{2,1,0:T(8,128)(2,1)S(1)}, bf16[1,1024,512]{2,1,0:T(8,128)(2,1)}, u32[]{:S(2)}) copy-start(bf16[1,1024,512]{2,1,0:T(8,128)(2,1)} %param.10) | copy-start | bytes 3145732
  7.2 6.2 %copy-start.1 = (bf16[576,512]{1,0:T(8,128)(2,1)S(1)}, bf16[576,512]{1,0:T(8,128)(2,1)}, u32[]{:S(2)}) copy-start(bf16[576,512]{1,0:T(8,128)(2,1)} %param.7) | copy-start | bytes 1769476
  8.6 30.6 %copy-start.7 = (bf16[576]{0:T(1024)(128)(2,1)S(1)}, bf16[576]{0:T(1024)(128)(2,1)}, u32[]{:S(2)}) copy-start(bf16[576]{0:T(1024)(128)(2,1)} %param.12) | copy-start | bytes 3460
  8.6 30.6 %copy-start.4 = (bf16[576,512]{1,0:T(8,128)(2,1)S(1)}, bf16[576,512]{1,0:T(8,128)(2,1)}, u32[]{:S(2)}) copy-start(bf16[576,512]{1,0:T(8,128)(2,1)} %param.13) | copy-start | bytes 1769476
  20.9 57.0 %all-to-all-start.1 = ((bf16[32,24,512]{2,1,0:T(8,128)(2,1)}), bf16[32,24,512]{2,1,0:T(8,128)(2,1)S(1)}, u32[]{:S(2)}, u32[]{:S(2)}) async-start(bf16[32,24,512]{2,1,0:T(8,128)(2,1)} %bitcast.52), calls=%async_computation.1 | async-start | bytes 1572864 | tf_op jit(solution)/shard_map/all_to_all | solution.py:65
  77.8 12.7 %copy-start.3 = (bf16[32,24,512]{2,1,0:T(8,128)(2,1)}, bf16[32,24,512]{2,1,0:T(8,128)(2,1)S(1)}, u32[]{:S(2)}) copy-start(bf16[32,24,512]{2,1,0:T(8,128)(2,1)S(1)} %all-to-all-done.1) | copy-start | bytes 2359300
  77.8 39.0 %all-to-all-start = ((bf16[32,24,512]{2,1,0:T(8,128)(2,1)}), bf16[32,24,512]{2,1,0:T(8,128)(2,1)}, u32[]{:S(2)}, u32[]{:S(2)}) async-start(bf16[32,24,512]{2,1,0:T(8,128)(2,1)} %bitcast.51), calls=%async_computation | async-start | bytes 1572864 | tf_op jit(solution)/shard_map/all_to_all | solution.py:66
  90.6 1.7 copy-start.2
  116.8 45.6 %all-to-all-start.3 = ((bf16[32,24,512]{2,1,0:T(8,128)(2,1)}), bf16[32,24,512]{2,1,0:T(8,128)(2,1)S(1)}, u32[]{:S(2)}, u32[]{:S(2)}) async-start(bf16[32,24,512]{2,1,0:T(8,128)(2,1)} %bitcast.54), calls=%async_computation.3 | async-start | bytes 1572864 | tf_op jit(solution)/shard_map/all_to_all | solution.py:88
  137.0 124.8 %reduce-scatter.5.cloned.1.call-start = ((), (), s32[]{:S(2)}) async-start(), calls=%async_computation.7 | async-start | bytes 1114112 | tf_op jit(solution)/shard_map/reduce_scatter | solution.py:106
  141.4 5.7 %copy-start.5 = (bf16[1,512,1024]{2,1,0:T(8,128)(2,1)S(1)}, bf16[1,512,1024]{2,1,0:T(8,128)(2,1)}, u32[]{:S(2)}) copy-start(bf16[1,512,1024]{2,1,0:T(8,128)(2,1)} %param.9) | copy-start | bytes 3145732
  146.0 1.2 copy-start.8
  162.4 194.8 %all-to-all-start.2 = ((bf16[32,24,512]{2,1,0:T(8,128)(2,1)}), bf16[32,24,512]{2,1,0:T(8,128)(2,1)S(1)}, u32[]{:S(2)}, u32[]{:S(2)}) async-start(bf16[32,24,512]{2,1,0:T(8,128)(2,1)} %bitcast.53), calls=%async_computation.2 | async-start | bytes 1572864 | tf_op jit(solution)/shard_map/all_to_all | solution.py:81
  182.5 168.0 %reduce-scatter.3.cloned.1.call-start = ((), (), s32[]{:S(2)}) async-start(), calls=%async_computation.6 | async-start | bytes 1114112 | tf_op jit(solution)/shard_map/reduce_scatter | solution.py:103
  357.3 2.8 copy-start.6
Sparse Core Ops, SparseCore 0:
  141.6 120.1 reduce-scatter.4
  264.8 85.5 reduce-scatter.2
where the time goes:
time: 371 us; the launch traced here: 370 us
  waiting for transfers between devices  228 us (61%)
  starting transfers between devices  69 us (19%)
  other arithmetic  30.5 us (8%)
  matrix products  18.7 us (5%)
  between operations  14.3 us (4%)
  local copies, waits for them, and re-layouts  9.09 us (2%)
    reduce_scatter x1, waiting for transfers between devices, body(): lax.psum_scatter(part_in.astype(jnp.bfloat16), 'dp', scatter_dimension=0,...  87.1 us
    reduce_scatter x1, waiting for transfers between devices, body(): lax.psum_scatter(part_out.astype(jnp.bfloat16), 'dp', scatter_dimension=0...  75.6 us
    all_to_all x1, waiting for transfers between devices, body(): lax.all_to_all(place_rows(normed), 'space', split_axis=0, concat_axis=0,...  29.6 us
    all_to_all x1, waiting for transfers between devices, body(): lax.all_to_all(place_rows(delta), 'space', split_axis=0, concat_axis=0, t...  22.5 us
    all_to_all x1, starting transfers between devices, body(): lax.all_to_all(token_out.reshape(sources, capacity, model_width), 'space'...  20.2 us
    all_to_all x1, starting transfers between devices, body(): lax.all_to_all(grad_normed.reshape(sources, capacity, model_width), 'spac...  20 us
    all_to_all x1, starting transfers between devices, body(): lax.all_to_all(place_rows(normed), 'space', split_axis=0, concat_axis=0,...  18.2 us
    scatter x2, other arithmetic, place_rows(): placed = blank_rows.at[target].set(rows, mode='drop')  16.6 us
  transfers between devices with their start and end apart: 6, of which 5 were waited for; matrix products, arithmetic and copies ran while one was open for 10% of the time, Pallas kernels for 0%

commit v1 on v0

v1 whole, which is shorter than its diff:
```python
import functools

import jax
import jax.numpy as jnp
from jax import lax
from jax.experimental import pallas as pl
from jax.experimental.pallas import tpu as pltpu
from jax.sharding import PartitionSpec as P

MESH = pl.DeviceIdType.MESH
F32 = jnp.float32
BF16 = jnp.bfloat16
EPS = 1e-05
CAP = 24
TOK = 576
D = 512
FF = 1024
ROWS = 32 * CAP
SLICE = FF // 16


def coordinates():
    space, group = lax.axis_index("space"), lax.axis_index("dp")
    return space // 8, group // 4, ((space // 2) % 4) * 4 + group % 4, space % 2


def device(x, y, z, c):
    return {"space": (x * 4 + z // 4) * 2 + c, "dp": y * 4 + z % 4}


def nt(left, right):
    return lax.dot_general(left, right, (((1,), (1,)), ((), ())), preferred_element_type=F32)


def tn(left, right):
    return lax.dot_general(left, right, (((0,), (0,)), ((), ())), preferred_element_type=F32)


def nn(left, right):
    return lax.dot_general(left, right, (((1,), (0,)), ((), ())), preferred_element_type=F32)


def iota(shape, dim):
    return lax.broadcasted_iota(jnp.int32, shape, dim).astype(F32)


def kernel(
    tok, gain, win, wout, ids, gate, gout,
    gtok, ggate, gwin, gwout,
    scaled_ref, col_ref, pair_ref, row_ref, sbuf, rbuf, xbuf, dbuf,
    wsend, wbuf, act_ref, gp_ref, dx_ref, gd_ref, gbuf, rl, rr,
    rt, bk, fsend, fout, pw, pout,
    disp_s, disp_r, ret_s, ret_r, pre_s, pre_r, ag_s, ag_r, rl_s, rl_r, rr_s, rr_r, fin_s, fin_r, fo_s, fo_r,
):
    x, y, z, c = coordinates()
    zh, zl = z // 4, z % 4
    me = x * 8 + y * 2 + c
    group = y * 4 + zl
    home = y == zh
    right, left = device(x, y, (z + 1) % 16, c), device(x, y, (z + 15) % 16, c)
    swap = device(x, zh, y * 4 + zl, c)

    barrier = pltpu.get_barrier_semaphore()

    def greet(to):
        pl.semaphore_signal(barrier, inc=1, device_id=to, device_id_type=MESH)

    def peer(j):
        px, py, pc = (x + j // 8) % 4, (y + (j // 2) % 4) % 4, (c + j) % 2
        return device(px, py, z, pc), px * 8 + py * 2 + pc

    greet(right)
    greet(left)

    @pl.loop(1, 32)
    def _(j):
        greet(peer(j)[0])

    @pl.loop(0, 16)
    def _(j):
        @pl.when(jnp.logical_not(home & (j == z)))
        def _():
            greet(device(x, zh, j, c))

    @pl.when(jnp.logical_not(home))
    def _():
        greet(swap)

    expert = ids[...].astype(F32)
    onehot = (expert == iota((TOK, 128), 1)).astype(F32)
    earlier = (iota((TOK, TOK), 0) > iota((TOK, TOK), 1)).astype(F32).astype(BF16)
    before = nn(earlier, onehot.astype(BF16))
    clipped = jnp.minimum(before, float(CAP)) * onehot
    rank = jnp.sum(clipped, axis=1, keepdims=True)
    kept = rank < float(CAP)
    expert_row = nt(iota((8, 128), 1).astype(BF16), onehot.astype(BF16))
    rank_row = nt(jnp.ones((8, 128), BF16), clipped.astype(BF16))
    row_ref[...] = jnp.where(rank_row < float(CAP), expert_row * float(CAP) + rank_row, -1.0)
    same = (iota((TOK, TOK), 0) == iota((TOK, TOK), 1)).astype(F32).astype(BF16)
    gate_col = nt(same, jnp.broadcast_to(gate[...], (8, TOK)))[:, 0:1]
    col_ref[...] = jnp.where(
        iota((TOK, 128), 1) == 0.0,
        expert,
        jnp.where(iota((TOK, 128), 1) == 1.0, rank, gate_col),
    )

    @pl.loop(0, 4)
    def _(i):
        at = pl.ds(pl.multiple_of(i * 144, 16), 144)
        values = tok[at, :].astype(F32)
        center = values - jnp.mean(values, axis=1, keepdims=True)
        spread = lax.rsqrt(jnp.mean(center * center, axis=1, keepdims=True) + EPS)
        scaled = center * spread
        scaled_ref[at, 0:D] = scaled
        scaled_ref[at, D : D + 128] = jnp.broadcast_to(spread, (144, 128))
        pair_ref[at, 0:D] = (scaled * gain[...]).astype(BF16)
        pair_ref[at, D : 2 * D] = (col_ref[at, 2:3] * gout[at, :].astype(F32)).astype(BF16)

    half = (group % 2).astype(F32)
    block = win[:, pl.ds(pl.multiple_of((group // 2) * 128, 128), 128)].astype(F32).T
    chosen = block[0:SLICE] * (1.0 - half) + block[SLICE : 2 * SLICE] * half
    wsend[0:SLICE, :] = chosen.astype(BF16)
    wsend[SLICE : 2 * SLICE, :] = wout[pl.ds(pl.multiple_of(group * SLICE, SLICE), SLICE), :]

    pl.semaphore_wait(barrier, jnp.where(home, 48, 50))

    pre = pltpu.make_async_remote_copy(
        src_ref=wsend, dst_ref=wbuf.at[group], send_sem=pre_s, recv_sem=pre_r,
        device_id=swap, device_id_type=MESH,
    )

    @pl.when(jnp.logical_not(home))
    def _():
        pre.start()

    @pl.when(home)
    def _():
        wbuf[group] = wsend[...]

    def dispatch(j):
        to, index = peer(j)
        return pltpu.make_async_remote_copy(
            src_ref=sbuf.at[index], dst_ref=rbuf.at[me], send_sem=disp_s.at[j], recv_sem=disp_r.at[j],
            device_id=to, device_id_type=MESH,
        )

    @pl.loop(0, 4)
    def _(i):
        dx = (i + 1) % 4
        first = ((x + dx) % 4) * 8
        slots = iota((8 * CAP, TOK), 0) + (first * CAP).astype(F32)
        chosen = (slots == row_ref[0:1, :]).astype(F32).astype(BF16)
        placed = nn(chosen, pair_ref[...])
        for e in range(8):
            rows = placed[e * CAP : (e + 1) * CAP]
            sbuf[first + e] = jnp.concatenate([rows[:, 0:D], rows[:, D : 2 * D]], axis=0).astype(BF16)

        @pl.loop(jnp.where(dx == 0, 1, 0), 8)
        def _(j):
            dispatch(dx * 8 + j).start()

    rbuf[me] = sbuf[me]

    def gather(a, h, way):
        return pltpu.make_async_remote_copy(
            src_ref=wbuf.at[a, pl.ds(h * SLICE, SLICE)], dst_ref=wbuf.at[a, pl.ds(h * SLICE, SLICE)],
            send_sem=ag_s.at[way, a, h], recv_sem=ag_r.at[a, h],
            device_id=(right, left)[way], device_id_type=MESH,
        )

    @pl.when(jnp.logical_not(home))
    def _():
        pltpu.make_async_remote_copy(
            src_ref=wsend, dst_ref=wbuf.at[z], send_sem=pre_s, recv_sem=pre_r,
            device_id=swap, device_id_type=MESH,
        ).wait_recv()

    for h in range(2):
        gather(z, h, 0).start()
        gather(z, h, 1).start()

    def hop(k):
        a, b = (z + 16 - k) % 16, (z + k) % 16
        for h in range(2):
            gather(a, h, 0).wait_recv()

            @pl.when(k < 8)
            def _(h=h):
                gather(a, h, 0).start()
                gather(b, h, 1).wait_recv()

                @pl.when(k < 7)
                def _():
                    gather(b, h, 1).start()

    @pl.loop(1, 5)
    def _(k):
        hop(k)

    @pl.loop(0, 16)
    def _(m):
        dx, dy = m // 4, m % 4
        for dc in range(2):
            @pl.when(m * 2 + dc > 0)
            def _(dc=dc):
                dispatch(m * 2 + dc).wait_recv()

        sx, sy = (x + 4 - dx) % 4, (y + 4 - dy) % 4
        n = sx * 4 + sy
        one, two = rbuf[n * 2].astype(F32), rbuf[n * 2 + 1].astype(F32)
        xbuf[n] = jnp.concatenate([one[0:CAP], two[0:CAP]], axis=0).astype(BF16)
        dbuf[n] = jnp.concatenate([one[CAP : 2 * CAP], two[CAP : 2 * CAP]], axis=0).astype(BF16)

    def reduce_left(s, h, src):
        return pltpu.make_async_remote_copy(
            src_ref=src.at[pl.ds(h * SLICE, SLICE)], dst_ref=rl.at[s, pl.ds(h * SLICE, SLICE)],
            send_sem=rl_s.at[s, h], recv_sem=rl_r.at[s, h], device_id=left, device_id_type=MESH,
        )

    def reduce_right(s, h, src):
        return pltpu.make_async_remote_copy(
            src_ref=src.at[pl.ds(h * SLICE, SLICE)], dst_ref=rr.at[s, pl.ds(h * SLICE, SLICE)],
            send_sem=rr_s.at[s, h], recv_sem=rr_r.at[s, h], device_id=right, device_id_type=MESH,
        )

    def reduce_step(s):
        for h in range(2):
            at = pl.ds(h * SLICE, SLICE)

            @pl.when(s == 0)
            def _(h=h):
                reduce_left(0, h, gbuf.at[0]).start()
                reduce_right(0, h, gbuf.at[1]).start()

            @pl.when(s > 0)
            def _(h=h, at=at):
                reduce_left(s - 1, h, gbuf.at[0]).wait_recv()
                rl[s - 1, at] = (rl[s - 1, at].astype(F32) + gbuf[2 * s, at].astype(F32)).astype(BF16)
                reduce_left(s, h, rl.at[s - 1]).start()

            @pl.when((s > 0) & (s < 7))
            def _(h=h, at=at):
                reduce_right(s - 1, h, gbuf.at[0]).wait_recv()
                rr[s - 1, at] = (rr[s - 1, at].astype(F32) + gbuf[2 * s + 1, at].astype(F32)).astype(BF16)
                reduce_right(s, h, rr.at[s - 1]).start()

    @pl.loop(0, 4)
    def _(g):
        hop(g + 5)
        held = [(z + 2 * g) % 16, (z + 15 - 2 * g) % 16, (z + 2 * g + 1) % 16, (z + 14 - 2 * g) % 16]
        w_in = jnp.concatenate([wbuf[a, 0:SLICE] for a in held], axis=0)
        w_out = jnp.concatenate([wbuf[a, SLICE : 2 * SLICE] for a in held], axis=0)

        @pl.loop(0, 4)
        def _(i):
            four = pl.ds(i * 4, 4)
            at = pl.ds(pl.multiple_of(i * 192, 16), 192)
            pre_act = nt(xbuf[four].reshape(192, D), w_in)
            grad_act = nt(dbuf[four].reshape(192, D), w_out)
            square = pre_act * pre_act
            curve = jnp.tanh(0.7978845608028654 * pre_act * (1.0 + 0.044715 * square))
            half_up = 0.5 * (1.0 + curve)
            activity = (pre_act * half_up).astype(BF16)
            slope = half_up + 0.5 * pre_act * (1.0 - curve * curve) * (
                0.7978845608028654 * (1.0 + 3 * 0.044715 * square)
            )
            grad_pre = (grad_act * slope).astype(BF16)
            act_ref[at, :] = activity
            gp_ref[at, :] = grad_pre
            dot = jnp.sum(activity.astype(F32) * grad_act, axis=1, keepdims=True)
            back = nn(grad_pre, w_in)

            @pl.when(g == 0)
            def _():
                gd_ref[at, :] = jnp.broadcast_to(dot, (192, 128))
                dx_ref[at, :] = back

            @pl.when(g > 0)
            def _():
                gd_ref[at, :] += jnp.broadcast_to(dot, (192, 128))
                dx_ref[at, :] += back

        part_in = tn(gp_ref[...], xbuf[...].reshape(ROWS, D)).astype(BF16)
        part_out = tn(act_ref[...], dbuf[...].reshape(ROWS, D)).astype(BF16)
        for j in range(4):
            gbuf[4 * g + j, 0:SLICE] = part_in[j * SLICE : (j + 1) * SLICE]
            gbuf[4 * g + j, SLICE : 2 * SLICE] = part_out[j * SLICE : (j + 1) * SLICE]
        reduce_step(2 * g)

        @pl.when(g < 3)
        def _():
            reduce_step(2 * g + 1)

    place = iota((ROWS, 128), 0) - jnp.floor(iota((ROWS, 128), 0) * (1.0 / CAP) + 0.5 / CAP) * CAP
    lane = iota((ROWS, 128), 1)
    total = gd_ref[...]
    high = total.astype(BF16).astype(F32)
    spread_out = jnp.where(lane == place, high, jnp.where(lane == place + 32.0, total - high, 0.0)).astype(BF16)
    owner = iota((32, ROWS), 1) - iota((32, ROWS), 0) * CAP
    pick = ((owner >= 0.0) & (owner < float(CAP))).astype(F32).astype(BF16)
    gd_ref[0:32, :] = nn(pick, spread_out)

    def give_back(j):
        to, index = peer(j)
        return pltpu.make_async_remote_copy(
            src_ref=rt.at[index], dst_ref=bk.at[me], send_sem=ret_s.at[j], recv_sem=ret_r.at[j],
            device_id=to, device_id_type=MESH,
        )

    @pl.loop(0, 32)
    def _(j):
        index = peer(j)[1]
        rows = dx_ref[pl.ds(pl.multiple_of(index * CAP, 8), CAP), :]
        extra = jnp.broadcast_to(gd_ref[pl.ds(index, 1), :], (8, 128))
        extra = jnp.concatenate([extra, jnp.zeros((8, D - 128), F32)], axis=1)
        rt[index] = jnp.concatenate([rows, extra], axis=0).astype(BF16)

        @pl.when(j > 0)
        def _():
            give_back(j).start()

    bk[me] = rt[me]

    reduce_step(jnp.int32(7))

    for h in range(2):
        reduce_left(7, h, gbuf.at[0]).wait_recv()
        reduce_right(6, h, gbuf.at[0]).wait_recv()
    summed = rl[7].astype(F32) + rr[6].astype(F32) + gbuf[15].astype(F32)
    fout[...] = summed[SLICE : 2 * SLICE].astype(BF16)
    turned = summed[0:SLICE].T.reshape(16, 32, SLICE)
    fsend[...] = jnp.concatenate([turned[:, 0:16], turned[:, 16:32]], axis=2).astype(BF16)

    def keep_in(j):
        return pltpu.make_async_remote_copy(
            src_ref=fsend.at[j], dst_ref=pw.at[z], send_sem=fin_s.at[j], recv_sem=fin_r.at[z],
            device_id=device(x, j // 4, y * 4 + j % 4, c), device_id_type=MESH,
        )

    def came_in(j):
        return pltpu.make_async_remote_copy(
            src_ref=fsend.at[j], dst_ref=pw.at[j], send_sem=fin_s.at[j], recv_sem=fin_r.at[j],
            device_id=right, device_id_type=MESH,
        )

    kept_slice = (z + 8) % 16
    keep_out = pltpu.make_async_remote_copy(
        src_ref=fout, dst_ref=pout, send_sem=fo_s, recv_sem=fo_r,
        device_id=device(x, kept_slice // 4, y * 4 + kept_slice % 4, c), device_id_type=MESH,
    )
    keep_out.start()

    @pl.loop(0, 16)
    def _(j):
        here = home & (j == group)

        @pl.when(jnp.logical_not(here))
        def _():
            keep_in(j).start()

        @pl.when(here)
        def _():
            pw[z] = fsend[j]

    @pl.loop(1, 32)
    def _(j):
        give_back(j).wait_recv()

    @pl.loop(0, 3)
    def _(i):
        at = pl.ds(pl.multiple_of(i * 192, 16), 192)
        expert, rank = col_ref[at, 0:1], col_ref[at, 1:2]
        kept = rank < float(CAP)
        slot = iota((192, 1024), 1)
        returned = bk[...].reshape(1024, D)
        chosen = (slot == jnp.where(kept, expert * 32.0 + rank, -1.0)).astype(F32).astype(BF16)
        token_grad = nn(chosen, returned)
        line = (slot == expert * 32.0 + float(CAP)).astype(F32).astype(BF16)
        products = nn(line, returned[:, 0:128])
        lane = iota((192, 128), 1)
        product = jnp.sum(
            jnp.where((lane == rank) | (lane == rank + 32.0), products, 0.0), axis=1, keepdims=True
        )
        scaled, spread = scaled_ref[at, 0:D], scaled_ref[at, D : D + 1]
        u = token_grad * gain[...]
        mean = jnp.mean(u, axis=1, keepdims=True)
        cross = jnp.mean(u * scaled, axis=1, keepdims=True)
        branch = jnp.where(kept, spread * (u - mean - scaled * cross), 0.0)
        gtok[at, :] = (gout[at, :].astype(F32) + branch).astype(BF16)
        answer = jnp.where(kept, product / col_ref[at, 2:3], 0.0)
        top = answer.astype(BF16).astype(F32)
        col_ref[at, :] = jnp.where(lane == 0.0, top, jnp.where(lane == 1.0, answer - top, 0.0))

    ggate[...] = nt(jnp.ones((8, 128), BF16), col_ref[...].astype(BF16))[0:1, :].astype(BF16)

    for j in range(8):
        wide = []
        for f in (2 * j, 2 * j + 1):
            at = (f + 8) % 16

            @pl.when(jnp.logical_not(home & (z == at)))
            def _(at=at):
                came_in(at).wait_recv()

            wide.append(pw[at].astype(F32))
        upper = jnp.concatenate([wide[0][:, 0:SLICE], wide[1][:, 0:SLICE]], axis=1)
        lower = jnp.concatenate([wide[0][:, SLICE : 2 * SLICE], wide[1][:, SLICE : 2 * SLICE]], axis=1)
        gwin[0:16, j * 128 : (j + 1) * 128] = upper
        gwin[16:32, j * 128 : (j + 1) * 128] = lower
    keep_out.wait_recv()
    gwout[...] = pout[...].astype(F32)

    @pl.when(jnp.logical_not(home))
    def _():
        pre.wait_send()

    @pl.loop(1, 32)
    def _(j):
        dispatch(j).wait_send()
        give_back(j).wait_send()

    @pl.loop(0, 8)
    def _(k):
        for h in range(2):
            gather((z + 16 - k) % 16, h, 0).wait_send()
            reduce_left(k, h, gbuf.at[0]).wait_send()

            @pl.when(k < 7)
            def _(h=h):
                gather((z + k) % 16, h, 1).wait_send()
                reduce_right(k, h, gbuf.at[0]).wait_send()

    @pl.loop(0, 16)
    def _(j):
        @pl.when(jnp.logical_not(home & (j == group)))
        def _():
            keep_in(j).wait_send()

    keep_out.wait_send()


def body(tokens, gain, w_in, w_out, expert_ids, gate, grad_out):
    vmem = pl.BlockSpec(memory_space=pltpu.VMEM)
    dma = pltpu.SemaphoreType.DMA
    scratch = [
        ((TOK, D + 128), F32), ((TOK, 128), F32), ((TOK, 2 * D), BF16), ((8, TOK), F32),
        ((32, 2 * CAP, D), BF16), ((32, 2 * CAP, D), BF16), ((16, 2 * CAP, D), BF16), ((16, 2 * CAP, D), BF16),
        ((2 * SLICE, D), BF16), ((16, 2 * SLICE, D), BF16), ((ROWS, 4 * SLICE), BF16), ((ROWS, 4 * SLICE), BF16),
        ((ROWS, D), F32), ((ROWS, 128), F32), ((16, 2 * SLICE, D), BF16),
        ((8, 2 * SLICE, D), BF16), ((7, 2 * SLICE, D), BF16),
        ((32, 32, D), BF16), ((32, 32, D), BF16), ((16, 16, 128), BF16), ((SLICE, D), BF16),
        ((16, 16, 128), BF16), ((SLICE, D), BF16),
    ]
    semaphores = [
        dma((32,)), dma((32,)), dma((32,)), dma((32,)), dma, dma, dma((2, 16, 2)), dma((16, 2)),
        dma((8, 2)), dma((8, 2)), dma((7, 2)), dma((7, 2)), dma((16,)), dma((16,)), dma, dma,
    ]
    out = pl.pallas_call(
        kernel,
        out_shape=(
            jax.ShapeDtypeStruct((TOK, D), BF16),
            jax.ShapeDtypeStruct((1, TOK), BF16),
            jax.ShapeDtypeStruct((D // 16, FF), F32),
            jax.ShapeDtypeStruct((SLICE, D), F32),
        ),
        in_specs=[vmem] * 7,
        out_specs=(vmem,) * 4,
        scratch_shapes=[pltpu.VMEM(shape, kind) for shape, kind in scratch] + semaphores,
        compiler_params=pltpu.CompilerParams(
            collective_id=0, has_side_effects=True, vmem_limit_bytes=56 * 1024 * 1024
        ),
        cost_estimate=pl.CostEstimate(flops=5 * 10**9, bytes_accessed=6 * 10**6, transcendentals=10**6),
    )(tokens, gain.reshape(1, D), w_in[0], w_out[0], expert_ids, gate.reshape(1, TOK), grad_out)
    return out[0], out[1].reshape(TOK), out[2][None], out[3][None]


def solution(mesh):
    placed = (
        P(("space", "dp"), None),
        P(),
        P("space", None, None),
        P("space", None, None),
        P(("space", "dp"), None),
        P(("space", "dp")),
        P(("space", "dp"), None),
    )
    return jax.shard_map(
        body,
        mesh=mesh,
        in_specs=placed,
        out_specs=(
            P(("space", "dp"), None),
            P(("space", "dp")),
            P("space", "dp", None),
            P("space", "dp", None),
        ),
        check_vma=False,
    )
```

time: 371 us -> 127 us (0.34)
  the two profiles are of different devices: /device:TPU:2 before, /device:TPU:28 now
where the time goes in v1:
time: 127 us
  Pallas kernels  119 us (94%)
  local copies, waits for them, and re-layouts  6.46 us (5%)
    pallas_call x1, Pallas kernels, body(): pl.pallas_call(kernel, out_shape=(jax.ShapeDtypeStruct((TOK, D), BF16), j...  119 us
    unnamed x14, local copies, waits for them, and re-layouts  5.88 us

profile of v1, /device:TPU:28, one launch (start us, length us, event | category | flops | bytes accessed | tf_op | source)
XLA Modules:
  0.0 126.8 jit_solution(17113282231154967525)
XLA Ops:
  0.6 0.0 copy-start.4
  0.6 0.7 copy-done.4
  1.3 0.0 copy-start.2
  1.3 0.6 reshape.18.gate
  1.9 0.1 copy-done.2
  2.0 0.9 copy.11.ids
  2.9 119.1 %shard_map.102 = (bf16[576,512]{1,0:T(8,128)(2,1)}, bf16[1,576]{1,0:T(2,128)(2,1)}, f32[32,1024]{1,0:T(8,128)}, f32[64,512]{1,0:T(8,128)}) custom-call(bf16[576,512]{1,0:T(8,128)(2,1)} %tok.1, f32[1,512]{1,0:T(1,128)} %bitcast.9, bf16[512,1024]{1,0:T(8,128)(2,1)} %bitcast.7, bf16[1024,512]{1,0:T(8,128)(2,1)} %bitcast.8, s32[576,1]{1,0:T(8,128)} %copy.11.ids, ...), custom_call_target="tpu_custom_call" | custom-call | flops 5000000000 | bytes 6000000 | tf_op jit(solution)/shard_map/pallas_call | solution.py:458
  121.9 0.0 copy-start.3
  122.0 0.7 copy-done.3
  122.6 0.6 reduce
  123.2 0.0 copy-start.1
  123.2 2.0 %copy.15 = bf16[576,512]{1,0:T(8,128)(2,1)} copy(bf16[576,512]{1,0:T(8,128)(2,1)} %get-tuple-element.16) | data formatting | bytes 1179648
  125.2 0.0 copy-done.1
  125.2 0.0 copy-start
  125.2 0.7 copy.16
  125.8 0.3 copy-done
  126.1 0.7 copy.17
Async XLA Ops:
  0.6 0.7 copy-start.4
  1.3 0.7 copy-start.2
  121.9 0.7 copy-start.3
  123.2 2.0 %copy-start.1 = (f32[32,1024]{1,0:T(8,128)S(1)}, f32[32,1024]{1,0:T(8,128)}, u32[]{:S(2)}) copy-start(f32[32,1024]{1,0:T(8,128)} %get-tuple-element.10) | copy-start | bytes 393220
  125.2 1.0 copy-start

commit v2 on v1

--- a/solution.py
+++ b/solution.py
@@ -45,12 +45,13 @@
 
 
 def kernel(
-    tok, gain, win, wout, ids, gate, gout,
+    tok_hbm, gain, win, wout, ids, gate, gout_hbm,
     gtok, ggate, gwin, gwout,
-    scaled_ref, col_ref, pair_ref, row_ref, sbuf, rbuf, xbuf, dbuf,
+    tok, gout, blocks, wide, scaled_ref, col_ref, pair_ref, row_ref, sbuf, rbuf, xbuf, dbuf,
     wsend, wbuf, act_ref, gp_ref, dx_ref, gd_ref, gbuf, rl, rr,
-    rt, bk, fsend, fout, pw, pout,
-    disp_s, disp_r, ret_s, ret_r, pre_s, pre_r, ag_s, ag_r, rl_s, rl_r, rr_s, rr_r, fin_s, fin_r, fo_s, fo_r,
+    rt, bk, fsend, fout, mid_in, mid_out, pw, pout, gtok_v, gwin_v, gwout_v,
+    tok_c, gout_c, wide_c, disp_s, disp_r, ret_s, ret_r, pre_s, pre_r, ag_s, ag_r, rl_s, rl_r, rr_s, rr_r, fin_s, fin_r, fo_s, fo_r,
+    mi_s, mi_r, mo_s, mo_r,
 ):
     x, y, z, c = coordinates()
     zh, zl = z // 4, z % 4
@@ -58,7 +59,59 @@
     group = y * 4 + zl
     home = y == zh
     right, left = device(x, y, (z + 1) % 16, c), device(x, y, (z + 15) % 16, c)
-    swap = device(x, zh, y * 4 + zl, c)
+    away = jnp.logical_not(home)
+    offset = (z + 16 - 4 * y) % 16
+
+    into_tok = pltpu.make_async_copy(tok_hbm, tok, tok_c)
+    into_gout = pltpu.make_async_copy(gout_hbm, gout, gout_c)
+    into_tok.start()
+    into_gout.start()
+
+    def flip(v):
+        return v + 1 - 2 * (v % 2)
+
+    def slice_of(a, k):
+        return ((a // 4 + 6 - k) % 4) * 4 + flip(a % 4)
+
+    def plane_of(f, k):
+        return ((f // 4 + 2 + k) % 4) * 4 + flip(f % 4)
+
+    def block_in(n, a):
+        return pltpu.make_async_copy(
+            win.at[:, pl.ds(pl.multiple_of((a // 2) * 128, 128), 128)], blocks.at[n], wide_c.at[n]
+        )
+
+    def rows_in(n, a):
+        return pltpu.make_async_copy(
+            wout.at[pl.ds(pl.multiple_of(a * SLICE, SLICE), SLICE)], wsend.at[n, 1], wide_c.at[2 + n]
+        )
+
+    outer = (zl == 0) | (zl == 3)
+    column = jnp.where(zl == 3, y + 4 - zh, y + 6 - zh) % 4
+    reach = (jnp.where(column == 0, 4, column), jnp.where(column == 0, 8, column + 4))
+    aims = [jnp.where(zl == 3, z + r, z + 16 - r) % 16 for r in reach]
+    sends = [outer & (r <= 6) for r in reach]
+
+    for n in range(2):
+        @pl.when(sends[n])
+        def _(n=n):
+            block_in(n, slice_of(aims[n], zh)).start()
+            rows_in(n, slice_of(aims[n], zh)).start()
+
+    whole_in = pltpu.make_async_copy(win, wide, wide_c.at[4])
+
+    def home_rows(f):
+        return pltpu.make_async_copy(
+            wout.at[pl.ds(pl.multiple_of(f * SLICE, SLICE), SLICE)], wbuf.at[plane_of(f, y), 1], wide_c.at[5 + f]
+        )
+
+    @pl.when(home)
+    def _():
+        whole_in.start()
+
+        @pl.loop(0, 16)
+        def _(f):
+            home_rows(f).start()
 
     barrier = pltpu.get_barrier_semaphore()
 
@@ -69,40 +122,106 @@
         px, py, pc = (x + j // 8) % 4, (y + (j // 2) % 4) % 4, (c + j) % 2
         return device(px, py, z, pc), px * 8 + py * 2 + pc
 
-    greet(right)
-    greet(left)
-
     @pl.loop(1, 32)
     def _(j):
         greet(peer(j)[0])
 
-    @pl.loop(0, 16)
-    def _(j):
-        @pl.when(jnp.logical_not(home & (j == z)))
-        def _():
-            greet(device(x, zh, j, c))
-
-    @pl.when(jnp.logical_not(home))
-    def _():
-        greet(swap)
-
-    expert = ids[...].astype(F32)
+    @pl.loop(1, 16)
+    def _(j):
+        greet(device(x, y, (z + j) % 16, c))
+
+    near = jnp.where(offset < 10, offset - 3, 16 - offset)
+    giver = jnp.where(
+        offset < 10,
+        device(x, (y + near) % 4, (4 * y + 3) % 16, c)["space"],
+        device(x, (y + near + 2) % 4, 4 * y, c)["space"],
+    )
+    giver_group = jnp.where(offset < 10, ((y + near) % 4) * 4 + 3, ((y + near + 2) % 4) * 4)
+    giver = {"space": giver, "dp": giver_group}
+
+    @pl.when(away)
+    def _():
+        greet(giver)
+
+    def gather(a, h, way):
+        return pltpu.make_async_remote_copy(
+            src_ref=wbuf.at[a, h], dst_ref=wbuf.at[a, h],
+            send_sem=ag_s.at[way, a, h], recv_sem=ag_r.at[a, h],
+            device_id=(right, left)[way], device_id_type=MESH,
+        )
+
+    def pre(n):
+        return pltpu.make_async_remote_copy(
+            src_ref=wsend.at[n], dst_ref=wbuf.at[aims[n]], send_sem=pre_s.at[n], recv_sem=pre_r,
+            device_id=device(x, zh, aims[n], c), device_id_type=MESH,
+        )
+
+    for n in range(2):
+        @pl.when(sends[n])
+        def _(n=n):
+            block_in(n, slice_of(aims[n], zh)).wait()
+            rows_in(n, slice_of(aims[n], zh)).wait()
+            half = (slice_of(aims[n], zh) % 2).astype(F32)
+            turned = blocks[n].astype(F32).T
+            wsend[n, 0] = (turned[0:SLICE] * (1.0 - half) + turned[SLICE : 2 * SLICE] * half).astype(BF16)
+
+    @pl.when(home)
+    def _():
+        whole_in.wait()
+        for j in range(8):
+            turned = wide[:, j * 128 : (j + 1) * 128].astype(F32).T.astype(BF16)
+            wbuf[plane_of(2 * j, y), 0] = turned[0:SLICE]
+            wbuf[plane_of(2 * j + 1, y), 0] = turned[SLICE : 2 * SLICE]
+
+        @pl.loop(0, 16)
+        def _(f):
+            home_rows(f).wait()
+
+    aimed = jnp.where(sends[0], 1, 0) + jnp.where(sends[1], 1, 0)
+    pl.semaphore_wait(barrier, 46 + aimed)
+
+    for n in range(2):
+        @pl.when(sends[n])
+        def _(n=n):
+            pre(n).start()
+
+    @pl.when(home)
+    def _():
+        @pl.when(zl == 3)
+        def _():
+            @pl.loop(0, 8)
+            def _(k):
+                for h in range(2):
+                    gather((z + 16 - k) % 16, h, 0).start()
+
+        @pl.when(zl == 0)
+        def _():
+            @pl.loop(0, 7)
+            def _(k):
+                for h in range(2):
+                    gather((z + k) % 16, h, 1).start()
+
+    same = (iota((TOK, TOK), 0) == iota((TOK, TOK), 1)).astype(F32).astype(BF16)
+    lines = jnp.where(iota((8, TOK), 0) == 0.0, ids[...].astype(F32), gate[...].astype(F32).reshape(1, TOK))
+    columns = nt(same, lines.astype(BF16))
+    expert, gate_col = columns[:, 0:1], columns[:, 1:2]
     onehot = (expert == iota((TOK, 128), 1)).astype(F32)
     earlier = (iota((TOK, TOK), 0) > iota((TOK, TOK), 1)).astype(F32).astype(BF16)
     before = nn(earlier, onehot.astype(BF16))
     clipped = jnp.minimum(before, float(CAP)) * onehot
     rank = jnp.sum(clipped, axis=1, keepdims=True)
     kept = rank < float(CAP)
-    expert_row = nt(iota((8, 128), 1).astype(BF16), onehot.astype(BF16))
+    expert_row = ids[...].astype(F32)
     rank_row = nt(jnp.ones((8, 128), BF16), clipped.astype(BF16))
     row_ref[...] = jnp.where(rank_row < float(CAP), expert_row * float(CAP) + rank_row, -1.0)
-    same = (iota((TOK, TOK), 0) == iota((TOK, TOK), 1)).astype(F32).astype(BF16)
-    gate_col = nt(same, jnp.broadcast_to(gate[...], (8, TOK)))[:, 0:1]
     col_ref[...] = jnp.where(
         iota((TOK, 128), 1) == 0.0,
         expert,
         jnp.where(iota((TOK, 128), 1) == 1.0, rank, gate_col),
     )
+
+    into_tok.wait()
+    into_gout.wait()
 
     @pl.loop(0, 4)
     def _(i):
@@ -116,26 +235,41 @@
         pair_ref[at, 0:D] = (scaled * gain[...]).astype(BF16)
         pair_ref[at, D : 2 * D] = (col_ref[at, 2:3] * gout[at, :].astype(F32)).astype(BF16)
 
-    half = (group % 2).astype(F32)
-    block = win[:, pl.ds(pl.multiple_of((group // 2) * 128, 128), 128)].astype(F32).T
-    chosen = block[0:SLICE] * (1.0 - half) + block[SLICE : 2 * SLICE] * half
-    wsend[0:SLICE, :] = chosen.astype(BF16)
-    wsend[SLICE : 2 * SLICE, :] = wout[pl.ds(pl.multiple_of(group * SLICE, SLICE), SLICE), :]
-
-    pl.semaphore_wait(barrier, jnp.where(home, 48, 50))
-
-    pre = pltpu.make_async_remote_copy(
-        src_ref=wsend, dst_ref=wbuf.at[group], send_sem=pre_s, recv_sem=pre_r,
-        device_id=swap, device_id_type=MESH,
-    )
-
-    @pl.when(jnp.logical_not(home))
-    def _():
-        pre.start()
-
-    @pl.when(home)
-    def _():
-        wbuf[group] = wsend[...]
+    last_right, last_left = offset == 15, offset == 4
+
+    def own_slice():
+        pltpu.make_async_remote_copy(
+            src_ref=wsend.at[0], dst_ref=wbuf.at[z], send_sem=pre_s.at[0], recv_sem=pre_r,
+            device_id=right, device_id_type=MESH,
+        ).wait_recv()
+        for h in range(2):
+            @pl.when(jnp.logical_not(last_right))
+            def _(h=h):
+                gather(z, h, 0).start()
+
+            @pl.when(jnp.logical_not(last_left))
+            def _(h=h):
+                gather(z, h, 1).start()
+
+    def hop(k):
+        a, b = (z + 16 - k) % 16, (z + k) % 16
+
+        @pl.when(away)
+        def _():
+            for h in range(2):
+                gather(a, h, 0).wait_recv()
+
+                @pl.when((k < 8) & jnp.logical_not(last_right))
+                def _(h=h):
+                    gather(a, h, 0).start()
+
+                @pl.when(k < 8)
+                def _(h=h):
+                    gather(b, h, 1).wait_recv()
+
+                @pl.when((k < 7) & jnp.logical_not(last_left))
+                def _(h=h):
+                    gather(b, h, 1).start()
 
     def dispatch(j):
         to, index = peer(j)
@@ -146,6 +280,14 @@
 
     @pl.loop(0, 4)
     def _(i):
+        @pl.when((i == 1) & away)
+        def _():
+            own_slice()
+
+        @pl.when(i == 3)
+        def _():
+            hop(1)
+
         dx = (i + 1) % 4
         first = ((x + dx) % 4) * 8
         slots = iota((8 * CAP, TOK), 0) + (first * CAP).astype(F32)
@@ -161,41 +303,9 @@
 
     rbuf[me] = sbuf[me]
 
-    def gather(a, h, way):
-        return pltpu.make_async_remote_copy(
-            src_ref=wbuf.at[a, pl.ds(h * SLICE, SLICE)], dst_ref=wbuf.at[a, pl.ds(h * SLICE, SLICE)],
-            send_sem=ag_s.at[way, a, h], recv_sem=ag_r.at[a, h],
-            device_id=(right, left)[way], device_id_type=MESH,
-        )
-
-    @pl.when(jnp.logical_not(home))
-    def _():
-        pltpu.make_async_remote_copy(
-            src_ref=wsend, dst_ref=wbuf.at[z], send_sem=pre_s, recv_sem=pre_r,
-            device_id=swap, device_id_type=MESH,
-        ).wait_recv()
-
-    for h in range(2):
-        gather(z, h, 0).start()
-        gather(z, h, 1).start()
-
-    def hop(k):
-        a, b = (z + 16 - k) % 16, (z + k) % 16
-        for h in range(2):
-            gather(a, h, 0).wait_recv()
-
-            @pl.when(k < 8)
-            def _(h=h):
-                gather(a, h, 0).start()
-                gather(b, h, 1).wait_recv()
-
-                @pl.when(k < 7)
-                def _():
-                    gather(b, h, 1).start()
-
-    @pl.loop(1, 5)
-    def _(k):
-        hop(k)
+    hop(2)
+    hop(3)
+    hop(4)
 
     @pl.loop(0, 16)
     def _(m):
@@ -248,8 +358,8 @@
     def _(g):
         hop(g + 5)
         held = [(z + 2 * g) % 16, (z + 15 - 2 * g) % 16, (z + 2 * g + 1) % 16, (z + 14 - 2 * g) % 16]
-        w_in = jnp.concatenate([wbuf[a, 0:SLICE] for a in held], axis=0)
-        w_out = jnp.concatenate([wbuf[a, SLICE : 2 * SLICE] for a in held], axis=0)
+        w_in = jnp.concatenate([wbuf[a, 0] for a in held], axis=0)
+        w_out = jnp.concatenate([wbuf[a, 1] for a in held], axis=0)
 
         @pl.loop(0, 4)
         def _(i):
@@ -331,36 +441,83 @@
     turned = summed[0:SLICE].T.reshape(16, 32, SLICE)
     fsend[...] = jnp.concatenate([turned[:, 0:16], turned[:, 16:32]], axis=2).astype(BF16)
 
+    owner = (zh + 4 - y) % 4
+
+    def cross_in(p):
+        return pltpu.make_async_remote_copy(
+            src_ref=fsend.at[pl.ds(p * 4, 4)], dst_ref=mid_in.at[y], send_sem=mi_s.at[p], recv_sem=mi_r.at[y],
+            device_id=device(x, p, z, c), device_id_type=MESH,
+        )
+
+    def crossed_in(k):
+        return pltpu.make_async_remote_copy(
+            src_ref=mid_in.at[k], dst_ref=mid_in.at[k], send_sem=mi_s.at[k], recv_sem=mi_r.at[k],
+            device_id=right, device_id_type=MESH,
+        )
+
+    cross_out = pltpu.make_async_remote_copy(
+        src_ref=fout, dst_ref=mid_out, send_sem=mo_s, recv_sem=mo_r,
+        device_id=device(x, owner, z, c), device_id_type=MESH,
+    )
+
+    @pl.when(owner != y)
+    def _():
+        cross_out.start()
+
+    @pl.when(owner == y)
+    def _():
+        mid_out[...] = fout[...]
+
+    @pl.loop(0, 4)
+    def _(p):
+        @pl.when(p != y)
+        def _():
+            cross_in(p).start()
+
+        @pl.when(p == y)
+        def _():
+            mid_in[p] = fsend[pl.ds(p * 4, 4)]
+
     def keep_in(j):
         return pltpu.make_async_remote_copy(
-            src_ref=fsend.at[j], dst_ref=pw.at[z], send_sem=fin_s.at[j], recv_sem=fin_r.at[z],
-            device_id=device(x, j // 4, y * 4 + j % 4, c), device_id_type=MESH,
-        )
-
-    def came_in(j):
-        return pltpu.make_async_remote_copy(
-            src_ref=fsend.at[j], dst_ref=pw.at[j], send_sem=fin_s.at[j], recv_sem=fin_r.at[j],
+            src_ref=mid_in.at[j // 4, j % 4], dst_ref=pw.at[z], send_sem=fin_s.at[j], recv_sem=fin_r.at[z],
+            device_id=device(x, y, j, c), device_id_type=MESH,
+        )
+
+    def came_in(t):
+        return pltpu.make_async_remote_copy(
+            src_ref=pw.at[t], dst_ref=pw.at[t], send_sem=fin_s.at[t], recv_sem=fin_r.at[t],
             device_id=right, device_id_type=MESH,
         )
 
-    kept_slice = (z + 8) % 16
     keep_out = pltpu.make_async_remote_copy(
-        src_ref=fout, dst_ref=pout, send_sem=fo_s, recv_sem=fo_r,
-        device_id=device(x, kept_slice // 4, y * 4 + kept_slice % 4, c), device_id_type=MESH,
+        src_ref=mid_out, dst_ref=pout, send_sem=fo_s, recv_sem=fo_r,
+        device_id=device(x, y, owner * 4 + flip(zl), c), device_id_type=MESH,
     )
+
+    @pl.when(owner != y)
+    def _():
+        cross_out.wait_recv()
+
     keep_out.start()
 
     @pl.loop(0, 16)
     def _(j):
-        here = home & (j == group)
-
-        @pl.when(jnp.logical_not(here))
+        @pl.when((j % 4 == 0) & (j // 4 != y))
+        def _():
+            crossed_in(j // 4).wait_recv()
+
+        @pl.when(j != z)
         def _():
             keep_in(j).start()
 
-        @pl.when(here)
-        def _():
-            pw[z] = fsend[j]
+        @pl.when(j == z)
+        def _():
+            pw[z] = mid_in[zh, zl]
+
+    out_tok = pltpu.make_async_copy(gtok_v, gtok, tok_c)
+    out_win = pltpu.make_async_copy(gwin_v, gwin, gout_c)
+    out_wout = pltpu.make_async_copy(gwout_v, gwout, wide_c.at[4])
 
     @pl.loop(1, 32)
     def _(j):
@@ -386,33 +543,36 @@
         mean = jnp.mean(u, axis=1, keepdims=True)
         cross = jnp.mean(u * scaled, axis=1, keepdims=True)
         branch = jnp.where(kept, spread * (u - mean - scaled * cross), 0.0)
-        gtok[at, :] = (gout[at, :].astype(F32) + branch).astype(BF16)
+        gtok_v[at, :] = (gout[at, :].astype(F32) + branch).astype(BF16)
         answer = jnp.where(kept, product / col_ref[at, 2:3], 0.0)
         top = answer.astype(BF16).astype(F32)
         col_ref[at, :] = jnp.where(lane == 0.0, top, jnp.where(lane == 1.0, answer - top, 0.0))
 
     ggate[...] = nt(jnp.ones((8, 128), BF16), col_ref[...].astype(BF16))[0:1, :].astype(BF16)
 
+    out_tok.start()
+
+    @pl.loop(1, 16)
+    def _(j):
+        came_in((z + j) % 16).wait_recv()
+
     for j in range(8):
-        wide = []
-        for f in (2 * j, 2 * j + 1):
-            at = (f + 8) % 16
-
-            @pl.when(jnp.logical_not(home & (z == at)))
-            def _(at=at):
-                came_in(at).wait_recv()
-
-            wide.append(pw[at].astype(F32))
-        upper = jnp.concatenate([wide[0][:, 0:SLICE], wide[1][:, 0:SLICE]], axis=1)
-        lower = jnp.concatenate([wide[0][:, SLICE : 2 * SLICE], wide[1][:, SLICE : 2 * SLICE]], axis=1)
-        gwin[0:16, j * 128 : (j + 1) * 128] = upper
-        gwin[16:32, j * 128 : (j + 1) * 128] = lower
+        wide_rows = [
+            pw[((f // 4 + zh) % 4) * 4 + flip(f % 4)].astype(F32) for f in (2 * j, 2 * j + 1)
+        ]
+        upper = jnp.concatenate([wide_rows[0][:, 0:SLICE], wide_rows[1][:, 0:SLICE]], axis=1)
+        lower = jnp.concatenate([wide_rows[0][:, SLICE : 2 * SLICE], wide_rows[1][:, SLICE : 2 * SLICE]], axis=1)
+        gwin_v[0:16, j * 128 : (j + 1) * 128] = upper
+        gwin_v[16:32, j * 128 : (j + 1) * 128] = lower
+    out_win.start()
     keep_out.wait_recv()
-    gwout[...] = pout[...].astype(F32)
-
-    @pl.when(jnp.logical_not(home))
-    def _():
-        pre.wait_send()
+    gwout_v[...] = pout[...].astype(F32)
+    out_wout.start()
+
+    for n in range(2):
+        @pl.when(sends[n])
+        def _(n=n):
+            pre(n).wait_send()
 
     @pl.loop(1, 32)
     def _(j):
@@ -422,38 +582,67 @@
     @pl.loop(0, 8)
     def _(k):
         for h in range(2):
-            gather((z + 16 - k) % 16, h, 0).wait_send()
+            @pl.when(((offset > 3) & jnp.logical_not(last_right)) | (offset == 3))
+            def _(h=h):
+                gather((z + 16 - k) % 16, h, 0).wait_send()
+
+            @pl.when((k < 7) & (((offset > 3) & jnp.logical_not(last_left)) | (offset == 0)))
+            def _(h=h):
+                gather((z + k) % 16, h, 1).wait_send()
+
             reduce_left(k, h, gbuf.at[0]).wait_send()
 
             @pl.when(k < 7)
             def _(h=h):
-                gather((z + k) % 16, h, 1).wait_send()
                 reduce_right(k, h, gbuf.at[0]).wait_send()
 
     @pl.loop(0, 16)
     def _(j):
-        @pl.when(jnp.logical_not(home & (j == group)))
+        @pl.when(j != z)
         def _():
             keep_in(j).wait_send()
 
+        @pl.when((j < 4) & (j != y))
+        def _():
+            cross_in(j).wait_send()
+
+    @pl.when(owner != y)
+    def _():
+        cross_out.wait_send()
+
     keep_out.wait_send()
+    out_tok.wait()
+    out_win.wait()
+    out_wout.wait()
+
+
+def finish(tok, gate, win, wout, tok_out, gate_out, win_out, wout_out):
+    tok_out[...] = tok[...]
+    gate_out[...] = gate[0, :]
+    win_out[...] = win[...]
+    wout_out[...] = wout[...]
 
 
 def body(tokens, gain, w_in, w_out, expert_ids, gate, grad_out):
     vmem = pl.BlockSpec(memory_space=pltpu.VMEM)
+    hbm = pl.BlockSpec(memory_space=pl.ANY)
     dma = pltpu.SemaphoreType.DMA
     scratch = [
+        ((TOK, D), BF16), ((TOK, D), BF16), ((2, D, 128), BF16), ((D, FF), BF16),
         ((TOK, D + 128), F32), ((TOK, 128), F32), ((TOK, 2 * D), BF16), ((8, TOK), F32),
         ((32, 2 * CAP, D), BF16), ((32, 2 * CAP, D), BF16), ((16, 2 * CAP, D), BF16), ((16, 2 * CAP, D), BF16),
-        ((2 * SLICE, D), BF16), ((16, 2 * SLICE, D), BF16), ((ROWS, 4 * SLICE), BF16), ((ROWS, 4 * SLICE), BF16),
+        ((2, 2, SLICE, D), BF16), ((16, 2, SLICE, D), BF16), ((ROWS, 4 * SLICE), BF16), ((ROWS, 4 * SLICE), BF16),
         ((ROWS, D), F32), ((ROWS, 128), F32), ((16, 2 * SLICE, D), BF16),
         ((8, 2 * SLICE, D), BF16), ((7, 2 * SLICE, D), BF16),
         ((32, 32, D), BF16), ((32, 32, D), BF16), ((16, 16, 128), BF16), ((SLICE, D), BF16),
-        ((16, 16, 128), BF16), ((SLICE, D), BF16),
+        ((4, 4, 16, 128), BF16), ((SLICE, D), BF16),
+        ((16, 16, 128), BF16), ((SLICE, D), BF16), ((TOK, D), BF16), ((D // 16, FF), F32), ((SLICE, D), F32),
     ]
     semaphores = [
-        dma((32,)), dma((32,)), dma((32,)), dma((32,)), dma, dma, dma((2, 16, 2)), dma((16, 2)),
+        dma, dma, dma((21,)),
+        dma((32,)), dma((32,)), dma((32,)), dma((32,)), dma((2,)), dma, dma((2, 16, 2)), dma((16, 2)),
         dma((8, 2)), dma((8, 2)), dma((7, 2)), dma((7, 2)), dma((16,)), dma((16,)), dma, dma,
+        dma((4,)), dma((4,)), dma, dma,
     ]
     out = pl.pallas_call(
         kernel,
@@ -463,15 +652,26 @@
             jax.ShapeDtypeStruct((D // 16, FF), F32),
             jax.ShapeDtypeStruct((SLICE, D), F32),
         ),
-        in_specs=[vmem] * 7,
-        out_specs=(vmem,) * 4,
+        in_specs=[hbm, vmem, hbm, hbm, vmem, vmem, hbm],
+        out_specs=(hbm, vmem, hbm, hbm),
         scratch_shapes=[pltpu.VMEM(shape, kind) for shape, kind in scratch] + semaphores,
         compiler_params=pltpu.CompilerParams(
             collective_id=0, has_side_effects=True, vmem_limit_bytes=56 * 1024 * 1024
         ),
         cost_estimate=pl.CostEstimate(flops=5 * 10**9, bytes_accessed=6 * 10**6, transcendentals=10**6),
-    )(tokens, gain.reshape(1, D), w_in[0], w_out[0], expert_ids, gate.reshape(1, TOK), grad_out)
-    return out[0], out[1].reshape(TOK), out[2][None], out[3][None]
+    )(tokens, gain.reshape(1, D), w_in[0], w_out[0], expert_ids.reshape(1, TOK), gate, grad_out)
+    out = pl.pallas_call(
+        finish,
+        out_shape=(
+            jax.ShapeDtypeStruct((TOK, D), BF16),
+            jax.ShapeDtypeStruct((TOK,), BF16),
+            jax.ShapeDtypeStruct((D // 16, FF), F32),
+            jax.ShapeDtypeStruct((SLICE, D), F32),
+        ),
+        in_specs=[vmem] * 4,
+        out_specs=(vmem,) * 4,
+    )(*out)
+    return out[0], out[1], out[2][None], out[3][None]
 
 
 def solution(mesh):

time: 127 us -> 113 us (0.89)
  the two profiles are of different devices: /device:TPU:28 before, /device:TPU:22 now
where the time goes in v2:
time: 113 us
  Pallas kernels  112 us (99%)
    pallas_call x1, Pallas kernels, body(): pl.pallas_call(kernel, out_shape=(jax.ShapeDtypeStruct((TOK, D), BF16), j...  110 us

profile of v2, /device:TPU:22, one launch (start us, length us, event | category | flops | bytes accessed | tf_op | source)
XLA Modules:
  0.0 112.5 jit_solution(11002950593548779004)
XLA Ops:
  0.6 109.8 %shard_map.102 = (bf16[576,512]{1,0:T(8,128)(2,1)}, bf16[1,576]{1,0:T(2,128)(2,1)}, f32[32,1024]{1,0:T(8,128)}, f32[64,512]{1,0:T(8,128)}) custom-call(bf16[576,512]{1,0:T(8,128)(2,1)} %tok_hbm.1, f32[1,512]{1,0:T(1,128)} %bitcast.11, bf16[512,1024]{1,0:T(8,128)(2,1)} %bitcast.6, bf16[1024,512]{1,0:T(8,128)(2,1)} %bitcast.7, s32[1,576]{1,0:T(1,128)} %bitcast.10, ...), custom_call_target="tpu_custom_call" | custom-call | flops 5000000000 | bytes 6000000 | tf_op jit(solution)/shard_map/pallas_call | solution.py:647
  110.4 2.1 %shard_map.103 = (bf16[576,512]{1,0:T(8,128)(2,1)}, bf16[576]{0:T(1024)(128)(2,1)}, f32[32,1024]{1,0:T(8,128)}, f32[64,512]{1,0:T(8,128)}) custom-call(bf16[576,512]{1,0:T(8,128)(2,1)} %get-tuple-element.12.tok, bf16[1,576]{1,0:T(2,128)(2,1)} %get-tuple-element.13.gate, f32[32,1024]{1,0:T(8,128)} %get-tuple-element.14.win, f32[64,512]{1,0:T(8,128)} %get-tuple-element.15.wout), custom_call_target="tpu_custom_call" | custom-call | tf_op jit(solution)/shard_map/pallas_call | solution.py:663

commit v3 on v2

--- a/solution.py
+++ b/solution.py
@@ -150,9 +150,9 @@
             device_id=(right, left)[way], device_id_type=MESH,
         )
 
-    def pre(n):
-        return pltpu.make_async_remote_copy(
-            src_ref=wsend.at[n], dst_ref=wbuf.at[aims[n]], send_sem=pre_s.at[n], recv_sem=pre_r,
+    def pre(n, h):
+        return pltpu.make_async_remote_copy(
+            src_ref=wsend.at[n, h], dst_ref=wbuf.at[aims[n], h], send_sem=pre_s.at[n, h], recv_sem=pre_r.at[h],
             device_id=device(x, zh, aims[n], c), device_id_type=MESH,
         )
 
@@ -180,10 +180,11 @@
     aimed = jnp.where(sends[0], 1, 0) + jnp.where(sends[1], 1, 0)
     pl.semaphore_wait(barrier, 46 + aimed)
 
-    for n in range(2):
-        @pl.when(sends[n])
-        def _(n=n):
-            pre(n).start()
+    for h in range(2):
+        for n in range(2):
+            @pl.when(sends[n])
+            def _(n=n, h=h):
+                pre(n, h).start()
 
     @pl.when(home)
     def _():
@@ -238,11 +239,12 @@
     last_right, last_left = offset == 15, offset == 4
 
     def own_slice():
-        pltpu.make_async_remote_copy(
-            src_ref=wsend.at[0], dst_ref=wbuf.at[z], send_sem=pre_s.at[0], recv_sem=pre_r,
-            device_id=right, device_id_type=MESH,
-        ).wait_recv()
         for h in range(2):
+            pltpu.make_async_remote_copy(
+                src_ref=wsend.at[0, h], dst_ref=wbuf.at[z, h], send_sem=pre_s.at[0, h], recv_sem=pre_r.at[h],
+                device_id=right, device_id_type=MESH,
+            ).wait_recv()
+
             @pl.when(jnp.logical_not(last_right))
             def _(h=h):
                 gather(z, h, 0).start()
@@ -280,15 +282,7 @@
 
     @pl.loop(0, 4)
     def _(i):
-        @pl.when((i == 1) & away)
-        def _():
-            own_slice()
-
-        @pl.when(i == 3)
-        def _():
-            hop(1)
-
-        dx = (i + 1) % 4
+        dx = (2 + 3 * i) % 4
         first = ((x + dx) % 4) * 8
         slots = iota((8 * CAP, TOK), 0) + (first * CAP).astype(F32)
         chosen = (slots == row_ref[0:1, :]).astype(F32).astype(BF16)
@@ -303,9 +297,13 @@
 
     rbuf[me] = sbuf[me]
 
-    hop(2)
-    hop(3)
-    hop(4)
+    @pl.when(away)
+    def _():
+        own_slice()
+
+    @pl.loop(1, 5)
+    def _(k):
+        hop(k)
 
     @pl.loop(0, 16)
     def _(m):
@@ -356,7 +354,6 @@
 
     @pl.loop(0, 4)
     def _(g):
-        hop(g + 5)
         held = [(z + 2 * g) % 16, (z + 15 - 2 * g) % 16, (z + 2 * g + 1) % 16, (z + 14 - 2 * g) % 16]
         w_in = jnp.concatenate([wbuf[a, 0] for a in held], axis=0)
         w_out = jnp.concatenate([wbuf[a, 1] for a in held], axis=0)
@@ -395,11 +392,26 @@
         for j in range(4):
             gbuf[4 * g + j, 0:SLICE] = part_in[j * SLICE : (j + 1) * SLICE]
             gbuf[4 * g + j, SLICE : 2 * SLICE] = part_out[j * SLICE : (j + 1) * SLICE]
-        reduce_step(2 * g)
+
+        @pl.when(g == 0)
+        def _():
+            reduce_step(0)
+
+        @pl.when(g > 0)
+        def _():
+            reduce_step(2 * g - 1)
 
         @pl.when(g < 3)
         def _():
-            reduce_step(2 * g + 1)
+            hop(g + 5)
+
+        @pl.when(g > 0)
+        def _():
+            reduce_step(2 * g)
+
+        @pl.when(g == 2)
+        def _():
+            hop(8)
 
     place = iota((ROWS, 128), 0) - jnp.floor(iota((ROWS, 128), 0) * (1.0 / CAP) + 0.5 / CAP) * CAP
     lane = iota((ROWS, 128), 1)
@@ -433,14 +445,6 @@
 
     reduce_step(jnp.int32(7))
 
-    for h in range(2):
-        reduce_left(7, h, gbuf.at[0]).wait_recv()
-        reduce_right(6, h, gbuf.at[0]).wait_recv()
-    summed = rl[7].astype(F32) + rr[6].astype(F32) + gbuf[15].astype(F32)
-    fout[...] = summed[SLICE : 2 * SLICE].astype(BF16)
-    turned = summed[0:SLICE].T.reshape(16, 32, SLICE)
-    fsend[...] = jnp.concatenate([turned[:, 0:16], turned[:, 16:32]], axis=2).astype(BF16)
-
     owner = (zh + 4 - y) % 4
 
     def cross_in(p):
@@ -460,13 +464,14 @@
         device_id=device(x, owner, z, c), device_id_type=MESH,
     )
 
-    @pl.when(owner != y)
-    def _():
-        cross_out.start()
-
-    @pl.when(owner == y)
-    def _():
-        mid_out[...] = fout[...]
+    def summed(h):
+        at = pl.ds(h * SLICE, SLICE)
+        reduce_left(7, h, gbuf.at[0]).wait_recv()
+        reduce_right(6, h, gbuf.at[0]).wait_recv()
+        return rl[7, at].astype(F32) + rr[6, at].astype(F32) + gbuf[15, at].astype(F32)
+
+    turned = summed(0).T.reshape(16, 32, SLICE)
+    fsend[...] = jnp.concatenate([turned[:, 0:16], turned[:, 16:32]], axis=2).astype(BF16)
 
     @pl.loop(0, 4)
     def _(p):
@@ -477,6 +482,16 @@
         @pl.when(p == y)
         def _():
             mid_in[p] = fsend[pl.ds(p * 4, 4)]
+
+    fout[...] = summed(1).astype(BF16)
+
+    @pl.when(owner != y)
+    def _():
+        cross_out.start()
+
+    @pl.when(owner == y)
+    def _():
+        mid_out[...] = fout[...]
 
     def keep_in(j):
         return pltpu.make_async_remote_copy(
@@ -572,7 +587,8 @@
     for n in range(2):
         @pl.when(sends[n])
         def _(n=n):
-            pre(n).wait_send()
+            pre(n, 0).wait_send()
+            pre(n, 1).wait_send()
 
     @pl.loop(1, 32)
     def _(j):
@@ -640,7 +656,7 @@
     ]
     semaphores = [
         dma, dma, dma((21,)),
-        dma((32,)), dma((32,)), dma((32,)), dma((32,)), dma((2,)), dma, dma((2, 16, 2)), dma((16, 2)),
+        dma((32,)), dma((32,)), dma((32,)), dma((32,)), dma((2, 2)), dma((2,)), dma((2, 16, 2)), dma((16, 2)),
         dma((8, 2)), dma((8, 2)), dma((7, 2)), dma((7, 2)), dma((16,)), dma((16,)), dma, dma,
         dma((4,)), dma((4,)), dma, dma,
     ]

time: 113 us -> 109 us (0.965)
  the two profiles are of different devices: /device:TPU:22 before, /device:TPU:16 now
where the time goes in v3:
time: 109 us
  Pallas kernels  108 us (99%)
    pallas_call x1, Pallas kernels, body(): pl.pallas_call(kernel, out_shape=(jax.ShapeDtypeStruct((TOK, D), BF16), j...  106 us

profile of v3, /device:TPU:16, one launch (start us, length us, event | category | flops | bytes accessed | tf_op | source)
XLA Modules:
  0.0 108.7 jit_solution(298451810681522262)
XLA Ops:
  0.6 106.0 %shard_map.102 = (bf16[576,512]{1,0:T(8,128)(2,1)}, bf16[1,576]{1,0:T(2,128)(2,1)}, f32[32,1024]{1,0:T(8,128)}, f32[64,512]{1,0:T(8,128)}) custom-call(bf16[576,512]{1,0:T(8,128)(2,1)} %tok_hbm.1, f32[1,512]{1,0:T(1,128)} %bitcast.11, bf16[512,1024]{1,0:T(8,128)(2,1)} %bitcast.6, bf16[1024,512]{1,0:T(8,128)(2,1)} %bitcast.7, s32[1,576]{1,0:T(1,128)} %bitcast.10, ...), custom_call_target="tpu_custom_call" | custom-call | flops 5000000000 | bytes 6000000 | tf_op jit(solution)/shard_map/pallas_call | solution.py:663
  106.7 2.1 %shard_map.103 = (bf16[576,512]{1,0:T(8,128)(2,1)}, bf16[576]{0:T(1024)(128)(2,1)}, f32[32,1024]{1,0:T(8,128)}, f32[64,512]{1,0:T(8,128)}) custom-call(bf16[576,512]{1,0:T(8,128)(2,1)} %get-tuple-element.12.tok, bf16[1,576]{1,0:T(2,128)(2,1)} %get-tuple-element.13.gate, f32[32,1024]{1,0:T(8,128)} %get-tuple-element.14.win, f32[64,512]{1,0:T(8,128)} %get-tuple-element.15.wout), custom_call_target="tpu_custom_call" | custom-call | tf_op jit(solution)/shard_map/pallas_call | solution.py:679

commit v4 on v3

--- a/solution.py
+++ b/solution.py
@@ -17,6 +17,7 @@
 FF = 1024
 ROWS = 32 * CAP
 SLICE = FF // 16
+PART = SLICE // 2
 
 
 def coordinates():
@@ -162,14 +163,14 @@
             block_in(n, slice_of(aims[n], zh)).wait()
             rows_in(n, slice_of(aims[n], zh)).wait()
             half = (slice_of(aims[n], zh) % 2).astype(F32)
-            turned = blocks[n].astype(F32).T
+            turned = blocks[n].T.astype(F32)
             wsend[n, 0] = (turned[0:SLICE] * (1.0 - half) + turned[SLICE : 2 * SLICE] * half).astype(BF16)
 
     @pl.when(home)
     def _():
         whole_in.wait()
         for j in range(8):
-            turned = wide[:, j * 128 : (j + 1) * 128].astype(F32).T.astype(BF16)
+            turned = wide[:, j * 128 : (j + 1) * 128].T
             wbuf[plane_of(2 * j, y), 0] = turned[0:SLICE]
             wbuf[plane_of(2 * j + 1, y), 0] = turned[SLICE : 2 * SLICE]
 
@@ -321,19 +322,19 @@
 
     def reduce_left(s, h, src):
         return pltpu.make_async_remote_copy(
-            src_ref=src.at[pl.ds(h * SLICE, SLICE)], dst_ref=rl.at[s, pl.ds(h * SLICE, SLICE)],
+            src_ref=src.at[pl.ds(h * PART, PART)], dst_ref=rl.at[s, pl.ds(h * PART, PART)],
             send_sem=rl_s.at[s, h], recv_sem=rl_r.at[s, h], device_id=left, device_id_type=MESH,
         )
 
     def reduce_right(s, h, src):
         return pltpu.make_async_remote_copy(
-            src_ref=src.at[pl.ds(h * SLICE, SLICE)], dst_ref=rr.at[s, pl.ds(h * SLICE, SLICE)],
+            src_ref=src.at[pl.ds(h * PART, PART)], dst_ref=rr.at[s, pl.ds(h * PART, PART)],
             send_sem=rr_s.at[s, h], recv_sem=rr_r.at[s, h], device_id=right, device_id_type=MESH,
         )
 
     def reduce_step(s):
-        for h in range(2):
-            at = pl.ds(h * SLICE, SLICE)
+        for h in range(4):
+            at = pl.ds(h * PART, PART)
 
             @pl.when(s == 0)
             def _(h=h):
@@ -466,8 +467,9 @@
 
     def summed(h):
         at = pl.ds(h * SLICE, SLICE)
-        reduce_left(7, h, gbuf.at[0]).wait_recv()
-        reduce_right(6, h, gbuf.at[0]).wait_recv()
+        for part in (2 * h, 2 * h + 1):
+            reduce_left(7, part, gbuf.at[0]).wait_recv()
+            reduce_right(6, part, gbuf.at[0]).wait_recv()
         return rl[7, at].astype(F32) + rr[6, at].astype(F32) + gbuf[15, at].astype(F32)
 
     turned = summed(0).T.reshape(16, 32, SLICE)
@@ -606,11 +608,12 @@
             def _(h=h):
                 gather((z + k) % 16, h, 1).wait_send()
 
-            reduce_left(k, h, gbuf.at[0]).wait_send()
-
-            @pl.when(k < 7)
-            def _(h=h):
-                reduce_right(k, h, gbuf.at[0]).wait_send()
+            for part in (2 * h, 2 * h + 1):
+                reduce_left(k, part, gbuf.at[0]).wait_send()
+
+                @pl.when(k < 7)
+                def _(part=part):
+                    reduce_right(k, part, gbuf.at[0]).wait_send()
 
     @pl.loop(0, 16)
     def _(j):
@@ -657,7 +660,7 @@
     semaphores = [
         dma, dma, dma((21,)),
         dma((32,)), dma((32,)), dma((32,)), dma((32,)), dma((2, 2)), dma((2,)), dma((2, 16, 2)), dma((16, 2)),
-        dma((8, 2)), dma((8, 2)), dma((7, 2)), dma((7, 2)), dma((16,)), dma((16,)), dma, dma,
+        dma((8, 4)), dma((8, 4)), dma((7, 4)), dma((7, 4)), dma((16,)), dma((16,)), dma, dma,
         dma((4,)), dma((4,)), dma, dma,
     ]
     out = pl.pallas_call(

time: 109 us -> 108 us (level)
  no operation moved by 1% of the time
where the time goes in v4:
time: 108 us
  Pallas kernels  108 us (100%)
    pallas_call x1, Pallas kernels, body(): pl.pallas_call(kernel, out_shape=(jax.ShapeDtypeStruct((TOK, D), BF16), j...  106 us

profile of v4, /device:TPU:16, one launch (start us, length us, event | category | flops | bytes accessed | tf_op | source)
XLA Modules:
  0.0 108.3 jit_solution(2625212670166345907)
XLA Ops:
  0.6 105.6 %shard_map.102 = (bf16[576,512]{1,0:T(8,128)(2,1)}, bf16[1,576]{1,0:T(2,128)(2,1)}, f32[32,1024]{1,0:T(8,128)}, f32[64,512]{1,0:T(8,128)}) custom-call(bf16[576,512]{1,0:T(8,128)(2,1)} %tok_hbm.1, f32[1,512]{1,0:T(1,128)} %bitcast.11, bf16[512,1024]{1,0:T(8,128)(2,1)} %bitcast.6, bf16[1024,512]{1,0:T(8,128)(2,1)} %bitcast.7, s32[1,576]{1,0:T(1,128)} %bitcast.10, ...), custom_call_target="tpu_custom_call" | custom-call | flops 5000000000 | bytes 6000000 | tf_op jit(solution)/shard_map/pallas_call | solution.py:666
  106.2 2.1 %shard_map.103 = (bf16[576,512]{1,0:T(8,128)(2,1)}, bf16[576]{0:T(1024)(128)(2,1)}, f32[32,1024]{1,0:T(8,128)}, f32[64,512]{1,0:T(8,128)}) custom-call(bf16[576,512]{1,0:T(8,128)(2,1)} %get-tuple-element.12.tok, bf16[1,576]{1,0:T(2,128)(2,1)} %get-tuple-element.13.gate, f32[32,1024]{1,0:T(8,128)} %get-tuple-element.14.win, f32[64,512]{1,0:T(8,128)} %get-tuple-element.15.wout), custom_call_target="tpu_custom_call" | custom-call | tf_op jit(solution)/shard_map/pallas_call | solution.py:682
